TPU v7x, 32 devices: a whole 2x2x4 slice. The times are simulated.
32 devices in a mesh: row: 16 (over z, y, core), col: 2 (over x).
Axes of the slice: x: 2, y: 2, z: 4, core: 2. Of those that a mesh axis runs over, the one named last changes fastest.
Arguments:
- homolog_embedding: float32 [128, 128, 256], P(None, 'row'), may hold values from -6 to 6
- pair_features: float32 [128, 128, 128], P('row', 'col'), may hold values from -6 to 6
- first_operand_matrix: float32 [256, 32], replicated, may hold values from -0.375 to 0.375
- second_operand_matrix: float32 [256, 32], replicated, may hold values from -0.375 to 0.375
- outer_output_weight: float32 [1024, 128], replicated, may hold values from -2 to 2
- triangle_input_weight: float32 [128, 512], replicated, may hold values from -0.5 to 0.5
- output_gate_weight: float32 [128, 128], replicated, may hold values from -0.5 to 0.5
- triangle_output_weight: float32 [128, 128], replicated, may hold values from -0.5 to 0.5
Outputs:
- pair_out: float32 [128, 128, 128], P('row', 'col')
All inputs are finite; a program needn't handle non-finite values.
Results may differ from a plain program's by a relative error of at most 0.000057.
Values sent between devices are 32-bit elements; how exact they have to be, the bound alone decides.
A program may use at most 64 MiB of HBM per device.

v0:
```python
import jax
import jax.numpy as jnp
from jax import lax
from jax.sharding import PartitionSpec as P

epsilon = 1e-05
top_precision = lax.Precision.HIGHEST


def broadcast(value, axis, source):
    kept = jnp.where(lax.axis_index(axis) == source, value, 0).astype(value.dtype)
    return lax.psum(kept, axis)


def apply_layer_norm(values):
    average = jnp.mean(values, -1, keepdims=True)
    centred = values - average
    variance = jnp.mean(centred * centred, -1, keepdims=True)
    return centred * lax.rsqrt(variance + epsilon)


def per_device(
    homolog_embedding,
    pair_features,
    first_operand_matrix,
    second_operand_matrix,
    outer_output_weight,
    triangle_input_weight,
    output_gate_weight,
    triangle_output_weight,
):
    sequence_number = homolog_embedding.shape[0]
    row_count = pair_features.shape[0]
    col_count = pair_features.shape[1]
    owner_count = lax.axis_size("row") // lax.axis_size("col")
    column_index = lax.axis_index("col")
    normalized_input = apply_layer_norm(homolog_embedding)
    left_alignment_proj = jnp.einsum(
        "bxp,pg->bxg", normalized_input, first_operand_matrix, precision=top_precision
    )
    right_alignment_proj = jnp.einsum(
        "bxp,pg->bxg", normalized_input, second_operand_matrix, precision=top_precision
    )
    collected_rows = lax.all_gather(right_alignment_proj, "row", axis=1, tiled=True)
    right_factor_columns = lax.dynamic_slice_in_dim(
        collected_rows, column_index * col_count, col_count, 1
    )
    outer_product_total = (
        jnp.einsum(
            "emp,eqk->mqpk", left_alignment_proj, right_factor_columns, precision=top_precision
        )
        / sequence_number
    )
    flattened = outer_product_total.reshape(row_count, col_count, -1)
    pair_mid = pair_features + jnp.einsum(
        "ijf,fz->ijz", flattened, outer_output_weight, precision=top_precision
    )
    normed_pair = apply_layer_norm(pair_mid)
    hidden_width = triangle_output_weight.shape[0]
    projected = jnp.einsum(
        "ijz,zh->ijh", normed_pair, triangle_input_weight, precision=top_precision
    )
    left_edge = (
        jax.nn.sigmoid(projected[..., hidden_width : 2 * hidden_width])
        * projected[..., :hidden_width]
    )
    right_edge = (
        jax.nn.sigmoid(projected[..., 3 * hidden_width :])
        * projected[..., 2 * hidden_width : 3 * hidden_width]
    )
    gate_act = jax.nn.sigmoid(
        jnp.einsum("ijz,zy->ijy", normed_pair, output_gate_weight, precision=top_precision)
    )
    full_left, full_right = (
        lax.all_gather(left_edge, "col", axis=1, tiled=True),
        lax.all_gather(right_edge, "col", axis=1, tiled=True),
    )
    blocks_out = []
    for offset in range(owner_count):
        panel_rows = broadcast(full_right, "row", column_index * owner_count + offset)
        blocks_out.append(
            jnp.einsum("ikc,jkc->ijc", full_left, panel_rows, precision=top_precision)
        )
    mixed_edges = jnp.concatenate(blocks_out, 1)
    return pair_mid + gate_act * jnp.einsum(
        "ijc,cz->ijz",
        apply_layer_norm(mixed_edges),
        triangle_output_weight,
        precision=top_precision,
    )


def solution(mesh):
    placed = (P(None, "row", None), P("row", "col", None), P(), P(), P(), P(), P(), P())
    return jax.shard_map(
        per_device, mesh=mesh, in_specs=placed, out_specs=P("row", "col", None), check_vma=False
    )
```

profile of v0, /device:TPU:3, one launch (start us, length us, event | category | flops | bytes accessed | tf_op | source)
XLA Modules:
  0.0 251.8 jit_solution(11072109669364347365)
XLA Ops:
  6.5 1.6 reduce_sum.54
  8.1 1.6 multiply_reduce_fusion
  9.7 2.3 fusion.8
  13.0 1.0 fusion.6
  14.2 41.9 %all-gather.2.cloned.1.call-done = f32[128,128,32]{0,2,1:T(8,128)} async-done(((f32[128,8,32]{0,2,1:T(8,128)}), f32[128,128,32]{0,2,1:T(8,128)}) %all-gather.2.cloned.1.call-update) | async-done | bytes 2097168 | tf_op jit(solution)/shard_map/all_gather | solution.py:44
  56.1 10.0 %multiply_bitcast_fusion = f32[8,64,32,32]{2,3,0,1:T(8,128)} fusion(f32[128,128,32]{0,2,1:T(8,128)} %all-gather.2.cloned.1.call-done, s32[]{:T(128)S(6)} %select_n.53, f32[128,8,32]{0,2,1:T(8,128)S(1)} %copy.46), kind=kOutput, calls=%fused_computation | convolution fusion | flops 805830656 | bytes 3276804 | tf_op jit(solution)/shard_map/emp,eqk->mqpk/dot_general | solution.py:49
  66.1 8.8 %copy.47 = f32[8,64,32,32]{1,3,2,0:T(8,128)} copy(f32[8,64,32,32]{2,3,0,1:T(8,128)} %multiply_bitcast_fusion) | data formatting | bytes 4194304 | tf_op jit(solution)/shard_map/div | solution.py:49
  74.9 9.0 %fusion.40 = (f32[8,64]{1,0:T(8,128)S(1)}, f32[8,64,128]{2,1,0:T(8,128)S(1)}) fusion(f32[8,64,128]{2,1,0:T(8,128)S(1)} %copy-done.2, f32[8,64,1024]{1,2,0:T(8,128)} %bitcast.64, f32[1024,128]{1,0:T(8,128)S(1)} %copy-done), kind=kOutput, calls=%fused_computation.74 | convolution fusion | flops 805436928 | bytes 3147776 | tf_op jit(solution)/shard_map/ijf,fz->ijz/dot_general | solution.py:55
  84.2 1.0 fusion.24
  85.4 8.3 %all_gather.10 = f32[8,128,128]{2,1,0:T(8,128)S(1)} all-gather(f32[8,64,128]{2,1,0:T(8,128)S(1)} %get-tuple-element.14), channel_id=1, replica_groups=mesh['row'=16,'col'=2] {'col'}, dimensions={1}, use_global_device_ids=true | all-gather | bytes 786432 | tf_op jit(solution)/shard_map/all_gather | solution.py:76
  93.7 2.1 broadcast_select_fusion
  95.8 7.7 %all_gather.11 = f32[8,128,128]{2,1,0:T(8,128)S(1)} all-gather(f32[8,64,128]{2,1,0:T(8,128)S(1)} %get-tuple-element.13), channel_id=1, replica_groups=mesh['row'=16,'col'=2] {'col'}, dimensions={1}, use_global_device_ids=true | all-gather | bytes 786432 | tf_op jit(solution)/shard_map/all_gather | solution.py:75
  103.8 1.2 fusion.3
  105.0 103.2 %all-reduce.3.cloned.1.call-done = (f32[8,128,128]{2,1,0:T(8,128)}, f32[8,128,128]{2,1,0:T(8,128)}, f32[8,128,128]{2,1,0:T(8,128)}, f32[8,128,128]{2,1,0:T(8,128...) async-done(((f32[8,128,128]{2,1,0:T(8,128)}, f32[8,128,128]{2,1,0:T(8,128)}, f32[8,128,128]{2,1,0:T(8,128)}, ...) | async-done | bytes 4194320 | tf_op jit(solution)/shard_map/psum | solution.py:12
  208.1 1.3 copy.63
  209.4 1.3 copy.61
  210.7 1.0 convolution_bitcast_fusion
  211.7 1.0 convolution_bitcast_fusion.1
  212.6 1.3 copy.59
  213.9 1.0 convolution_bitcast_fusion.2
  214.9 2.1 copy.57
  216.9 2.0 convolution_bitcast_fusion.3
  218.9 2.0 copy.55
  221.0 2.8 %convolution_bitcast_fusion.4 = f32[8,8,128]{1,0,2:T(8,128)} fusion(f32[8,128,128]{1,0,2:T(8,128)} %copy.55, f32[8,128,128]{1,0,2:T(8,128)S(1)} %copy.50), kind=kOutput, calls=%fused_computation.5 | convolution fusion | flops 12582912 | bytes 1081344 | tf_op jit(solution)/shard_map/ikc,jkc->ijc/dot_general | solution.py:82
  223.8 2.0 copy.53
  225.8 2.8 %convolution_bitcast_fusion.5 = f32[8,8,128]{1,0,2:T(8,128)} fusion(f32[8,128,128]{1,0,2:T(8,128)} %copy.53, f32[8,128,128]{1,0,2:T(8,128)S(1)} %copy.50), kind=kOutput, calls=%fused_computation.6 | convolution fusion | flops 12582912 | bytes 1081344 | tf_op jit(solution)/shard_map/ikc,jkc->ijc/dot_general | solution.py:82
  228.7 2.0 copy.51
  230.7 2.8 %convolution_bitcast_fusion.6 = f32[8,8,128]{1,0,2:T(8,128)} fusion(f32[8,128,128]{1,0,2:T(8,128)} %copy.51, f32[8,128,128]{1,0,2:T(8,128)S(1)} %copy.50), kind=kOutput, calls=%fused_computation.7 | convolution fusion | flops 12582912 | bytes 1081344 | tf_op jit(solution)/shard_map/ikc,jkc->ijc/dot_general | solution.py:82
  233.5 2.0 copy.49
  235.5 2.8 %convolution_bitcast_fusion.7 = f32[8,8,128]{1,0,2:T(8,128)} fusion(f32[8,128,128]{1,0,2:T(8,128)} %copy.49, f32[8,128,128]{1,0,2:T(8,128)S(1)} %copy.50), kind=kOutput, calls=%fused_computation.8 | convolution fusion | flops 12582912 | bytes 1081344 | tf_op jit(solution)/shard_map/ikc,jkc->ijc/dot_general | solution.py:82
  238.4 3.6 %concatenate.3 = f32[8,64,128]{1,0,2:T(8,128)S(1)} concatenate(f32[8,8,128]{1,0,2:T(8,128)} %convolution_bitcast_fusion.7, f32[8,8,128]{1,0,2:T(8,128)} %convolution_bitcast_fusion.6, f32[8,8,128]{1,0,2:T(8,128)} %convolution_bitcast_fusion.5, f32[8,8,128]{1,0,2:T(8,128)} %convolution_bitcast_fusion.4, f32[8,8,128]{1,0,2:T(8,128)S(1)} %convolution_bitcast_fusion.3, ...), dimensions={1} | concatenate | bytes 524288 | tf_op jit(solution)/shard_map/concatenate | solution.py:84
  242.4 2.6 %fusion = f32[8,64,128]{2,1,0:T(8,128)} fusion(f32[8,64,128]{2,1,0:T(8,128)S(1)} %get-tuple-element.24, f32[8,64,128]{2,1,0:T(8,128)} %fusion.3, f32[8,64,128]{1,0,2:T(8,128)S(1)} %subtract_multiply_fusion, f32[128,128]{1,0:T(8,128)S(1)} %copy-done.4), kind=kOutput, calls=%fused_computation.10 | convolution fusion | flops 100794368 | bytes 1114112 | tf_op jit(solution)/shard_map/ijc,cz->ijz/dot_general | solution.py:85
  (32 shorter events, 2.2 us)
Async XLA Ops:
  6.5 68.4 %copy-start = (f32[1024,128]{1,0:T(8,128)S(1)}, f32[1024,128]{1,0:T(8,128)}, u32[]{:S(2)}) copy-start(f32[1024,128]{1,0:T(8,128)} %param.12) | copy-start | bytes 1572868
  6.5 6.4 %copy-start.1 = (f32[128,8,256]{2,1,0:T(8,128)S(1)}, f32[128,8,256]{2,1,0:T(8,128)}, u32[]{:S(2)}) copy-start(f32[128,8,256]{2,1,0:T(8,128)} %param.8) | copy-start | bytes 3145732
  6.5 6.4 %copy-start.6 = (f32[256,32]{0,1:T(8,128)S(1)}, f32[256,32]{0,1:T(8,128)}, u32[]{:S(2)}) copy-start(f32[256,32]{0,1:T(8,128)} %param.10) | copy-start | bytes 98308
  6.5 49.6 %all-gather.2.cloned.1.call-start = ((), (), s32[]{:S(2)}) async-start(), calls=%async_computation | async-start | bytes 2228224 | tf_op jit(solution)/shard_map/all_gather | solution.py:44
  12.9 195.2 %all-reduce.3.cloned.1.call-start = ((), (), s32[]{:S(2)}) async-start(), calls=%async_computation.1 | async-start | bytes 8388608 | tf_op jit(solution)/shard_map/psum | solution.py:12
  66.1 8.8 %copy-start.2 = (f32[8,64,128]{2,1,0:T(8,128)S(1)}, f32[8,64,128]{2,1,0:T(8,128)}, u32[]{:S(2)}) copy-start(f32[8,64,128]{2,1,0:T(8,128)} %param.9) | copy-start | bytes 786436
  74.9 9.3 %copy-start.3 = (f32[128,512]{1,0:T(8,128)S(1)}, f32[128,512]{1,0:T(8,128)}, u32[]{:S(2)}) copy-start(f32[128,512]{1,0:T(8,128)} %param.13) | copy-start | bytes 786436
  95.8 8.0 %copy-start.5 = (f32[128,128]{1,0:T(8,128)S(1)}, f32[128,128]{1,0:T(8,128)}, u32[]{:S(2)}) copy-start(f32[128,128]{1,0:T(8,128)} %param.14) | copy-start | bytes 196612
  235.5 6.8 %copy-start.4 = (f32[128,128]{1,0:T(8,128)S(1)}, f32[128,128]{1,0:T(8,128)}, u32[]{:S(2)}) copy-start(f32[128,128]{1,0:T(8,128)} %param.15) | copy-start | bytes 196612
Sparse Core Ops, SparseCore 0:
  13.0 43.0 all-gather.1
  95.9 112.1 all-reduce.2
where the time goes:
time: 255 us; the launch traced here: 252 us
  waiting for transfers between devices  145 us (57%)
  matrix products  43.3 us (17%)
  local copies, waits for them, and re-layouts  27.7 us (11%)
  blocking collectives  16.1 us (6%)
  between operations  13.6 us (5%)
  other arithmetic  5.98 us (2%)
    psum x1, waiting for transfers between devices, broadcast(): return lax.psum(kept, axis)  103 us
    all_gather x1, waiting for transfers between devices, per_device(): lax.all_gather(right_alignment_proj, 'row', axis=1, tiled=True)  41.9 us
    dot_general x8, matrix products, per_device(): jnp.einsum('ikc,jkc->ijc', full_left, panel_rows, precision=top_precision)  16.2 us
    psum x8, local copies, waits for them, and re-layouts, broadcast(): return lax.psum(kept, axis)  14 us
    dot_general x1, matrix products, per_device(): jnp.einsum('emp,eqk->mqpk', left_alignment_proj, right_factor_columns, pr...  10 us
    dot_general x1, matrix products, per_device(): jnp.einsum('ijf,fz->ijz', flattened, outer_output_weight, precision=top_p...  9 us
    div x1, local copies, waits for them, and re-layouts, per_device(): jnp.einsum('emp,eqk->mqpk', left_alignment_proj, right_factor_columns, pr...  8.76 us
    all_gather x1, blocking collectives, per_device(): lax.all_gather(right_edge, 'col', axis=1, tiled=True)  8.33 us
  transfers between devices with their start and end apart: 2, of which 2 were waited for; matrix products, arithmetic and copies ran while one was open for 1% of the time, Pallas kernels for 0%

commit v1 on v0

v1 whole, which is shorter than its diff:
```python
import functools

import jax
import jax.numpy as jnp
from jax import lax
from jax.experimental import pallas as pl
from jax.experimental.pallas import tpu as pltpu
from jax.sharding import PartitionSpec as P

epsilon = 1e-05
MESH = pl.DeviceIdType.MESH
f32 = jnp.float32
bf16 = jnp.bfloat16


def split(x):
    hi = x.astype(bf16)
    lo = (x - hi.astype(f32)).astype(bf16)
    return hi, lo


def dot_nn(a, b):
    return lax.dot_general(a, b, (((1,), (0,)), ((), ())), preferred_element_type=f32)


def dot_nt(a, b):
    return lax.dot_general(a, b, (((1,), (1,)), ((), ())), preferred_element_type=f32)


def layer_norm(values):
    average = jnp.mean(values, -1, keepdims=True)
    centred = values - average
    variance = jnp.mean(centred * centred, -1, keepdims=True)
    return centred * lax.rsqrt(variance + epsilon)


def sigmoid(x):
    return 1.0 / (1.0 + jnp.exp(-x))


def kernel(
    dims,
    msa_ref,
    pair_ref,
    first_ref,
    second_ref,
    outer_ref,
    tri_in_ref,
    gate_w_ref,
    tri_out_ref,
    out_ref,
    nm_ref,
    lt_ref,
    rt_ref,
    rg,
    wp_ref,
    x_ref,
    pm_ref,
    gate_ref,
    redge_ref,
    lall,
    rbuf,
    mst,
    accb,
    a_up,
    a_down,
    a_y,
    a_core,
    a_recv,
    l_sem,
    ring_cw,
    ring_ccw,
    ring_recv,
    m_send,
    m_recv,
):
    S, I, J, R, C, half, channels = dims
    nr = R // C
    Z = R // 4
    zs = nr // 4
    ring = R // 2
    rows = nr * 64

    r = lax.axis_index("row")
    c = lax.axis_index("col")
    core = lax.rem(r, 2)
    y = lax.rem(lax.div(r, 2), 2)
    z = lax.div(r, 4)
    pos = z + y * (ring - 1 - 2 * z)

    def row_at(zz, yy, cc):
        return zz * 4 + yy * 2 + cc

    def ring_row(q):
        q = lax.rem(q, ring)
        yy = lax.div(q, Z)
        zz = q * (1 - yy) + (ring - 1 - q) * yy
        return row_at(zz, yy, core)

    up_row = row_at(lax.rem(z + 1, Z), y, core)
    down_row = row_at(lax.rem(z + Z - 1, Z), y, core)
    y_row = row_at(z, 1 - y, core)
    core_row = row_at(z, y, 1 - core)

    barrier = pltpu.get_barrier_semaphore()
    greet = [(up_row, c), (down_row, c), (y_row, c), (core_row, c)]
    for d in range(1, C):
        other = lax.rem(c + d, C)
        greet += [(r, other), (core_row, other)]
    for target in greet:
        pl.semaphore_signal(barrier, inc=1, device_id=target, device_id_type=MESH)

    both = jnp.concatenate(
        [first_ref[...], second_ref[...], jnp.zeros((first_ref.shape[0], 128 - 2 * half), f32)], 1
    ).T
    both_h, both_l = split(both[: 2 * half])
    both_hl = jnp.concatenate([both_h, both_l], 0)
    depth = msa_ref.shape[1]
    normed = layer_norm(msa_ref[...])
    for n in range(depth // 128):
        nm_ref[n] = normed[:, n * 128 : (n + 1) * 128]
    for m in range(I):
        xh, xl = split(
            jnp.concatenate([nm_ref[n, pl.ds(m, S, stride=I), :] for n in range(depth // 128)], 1)
        )
        t = dot_nt(both_hl, xh)
        t = t[: 2 * half] + t[2 * half :] + dot_nt(both_h, xl)
        lt_ref[m * half : (m + 1) * half, :] = t[:half] * (1.0 / S)
        rt_ref[m * half : (m + 1) * half, :] = t[half:]

    @pl.when(lax.div(r, nr) == c)
    def _():
        slot = lax.rem(r, nr)
        for b in range(half):
            rg[slot, b * I : (b + 1) * I, :] = rt_ref[pl.ds(b, I, stride=half), :]

    pl.semaphore_wait(barrier, len(greet))

    def a_copy(slot, send, target):
        return pltpu.make_async_remote_copy(
            src_ref=rg.at[slot],
            dst_ref=rg.at[slot],
            send_sem=send,
            recv_sem=a_recv.at[slot],
            device_id=(target, c),
            device_id_type=MESH,
        )

    flip = (z > c * zs).astype(jnp.int32)

    def near(t):
        return t + flip * (zs - 1 - 2 * t)

    def a_links(t):
        zi = near(t)
        source = c * zs + zi
        slot = zi * 4 + y * 2 + core
        return (
            slot,
            source,
            jnp.logical_and(z >= source, z < Z - 1),
            jnp.logical_and(z <= source, z > 0),
        )

    for t in range(zs):
        slot, source, goes_up, goes_down = a_links(t)

        @pl.when(z != source)
        def _():
            a_copy(slot, a_y.at[t], y_row).wait_recv()

        @pl.when(goes_up)
        def _():
            a_copy(slot, a_up.at[t], up_row).start()

        @pl.when(goes_down)
        def _():
            a_copy(slot, a_down.at[t], down_row).start()

        a_copy(slot, a_y.at[t], y_row).start()
        a_copy(slot, a_core.at[t, 0], core_row).start()

    for b in range(half):
        wp_ref[b * half : (b + 1) * half, :] = outer_ref[pl.ds(b, half, stride=half), :]

    lt = lt_ref[...]
    lt_h, lt_l = split(lt)
    lt_hh = jnp.concatenate([lt_h, lt_h], 1)
    lane = lax.broadcasted_iota(jnp.int32, (half // 4, I, 128), 2)
    low64 = lane < 64
    low32 = lax.rem(lane, 64) < 32

    def outer_block(slot):
        rh, rl = split(rg[slot])
        o = dot_nt(jnp.concatenate([rh, rl], 1), lt_hh) + dot_nt(rh, lt_l)
        o = o.reshape(half // 4, 4, I, half * I)
        for h in range(half * I // 128):
            x = [o[:, q, :, h * 128 : (h + 1) * 128] for q in range(4)]
            w = [None] * 4
            for q in range(2):
                w[q] = jnp.where(low64, x[q], pltpu.roll(x[q + 2], 64, 2))
                w[q + 2] = jnp.where(low64, pltpu.roll(x[q], 64, 2), x[q + 2])
            v = [None] * 4
            for q in (0, 2):
                v[q] = jnp.where(low32, w[q], pltpu.roll(w[q + 1], 32, 2))
                v[q + 1] = jnp.where(low32, pltpu.roll(w[q], 96, 2), w[q + 1])
            for q in range(4):
                i = h * 4 + q
                for g in range(half // 4):
                    x_ref[slot, i * I : (i + 1) * I, g * 128 : (g + 1) * 128] = v[q][g]

    for t in range(zs):
        slot = a_links(t)[0]
        outer_block(slot)
    for t in range(zs):
        slot = near(t) * 4 + (1 - y) * 2 + core
        a_copy(slot, a_core.at[t, 1], core_row).wait_recv()
        a_copy(slot, a_core.at[t, 1], core_row).start()
    for t in range(zs):
        outer_block(near(t) * 4 + (1 - y) * 2 + core)
    for yy in range(2):
        for t in range(zs):
            slot = near(t) * 4 + lax.rem(y + yy, 2) * 2 + 1 - core
            a_copy(slot, a_core.at[t, 1], core_row).wait_recv()
            outer_block(slot)

    wh, wl = split(wp_ref[...])
    w_hl = jnp.concatenate([wh, wl], 1)
    in_w = jnp.concatenate([tri_in_ref[...], gate_w_ref[...]], 1)
    in_h, in_l = split(in_w)
    in_hh = jnp.concatenate([in_h, in_h], 0)
    chunk_slots = min(4, nr)
    chunk = chunk_slots * 64
    for n in range(nr // chunk_slots):
        xh, xl = split(x_ref[n * chunk_slots : (n + 1) * chunk_slots].reshape(chunk, half * half))
        t = dot_nn(xh, w_hl)
        t = t[:, :channels] + t[:, channels:] + dot_nn(xl, wh)
        own = jnp.concatenate(
            [
                pair_ref[i * J + s * I : i * J + (s + 1) * I, :]
                for s in range(n * chunk_slots, (n + 1) * chunk_slots)
                for i in range(I)
            ],
            0,
        )
        mid = own + t
        sl = pl.ds(n * chunk, chunk)
        pm_ref[sl, :] = mid
        nh, nl = split(layer_norm(mid))
        pr = dot_nn(jnp.concatenate([nh, nl], 1), in_hh) + dot_nn(nh, in_l)
        ch = tri_out_ref.shape[0]
        lall[core, sl, :] = sigmoid(pr[:, ch : 2 * ch]) * pr[:, :ch]
        redge_ref[sl, :] = sigmoid(pr[:, 3 * ch : 4 * ch]) * pr[:, 2 * ch : 3 * ch]
        gate_ref[sl, :] = sigmoid(pr[:, 4 * ch :])

    for s in range(nr):
        for k in range(I):
            at = (s * I + k) * I
            rbuf[0, at : at + I, :] = redge_ref[pl.ds(s * 64 + k, I, stride=I), :]

    part = rows // 2

    def ring_copy(src, dst, h, send, target):
        return pltpu.make_async_remote_copy(
            src_ref=rbuf.at[src, pl.ds(h * part, part)],
            dst_ref=rbuf.at[dst, pl.ds(h * part, part)],
            send_sem=send,
            recv_sem=ring_recv.at[dst, h],
            device_id=(target, c),
            device_id_type=MESH,
        )

    next_row = ring_row(pos + 1)
    prev_row = ring_row(pos + ring - 1)
    far = ring // 2

    def cw(t, h):
        return ring_copy(t, t + 1, h, ring_cw.at[t, h], next_row)

    def ccw(t, h):
        return ring_copy((ring - t) % ring, ring - t - 1, h, ring_ccw.at[t, h], prev_row)

    l_copy = pltpu.make_async_remote_copy(
        src_ref=lall.at[core],
        dst_ref=lall.at[core],
        send_sem=l_sem.at[0],
        recv_sem=l_sem.at[1],
        device_id=(core_row, c),
        device_id_type=MESH,
    )

    def forward(t):
        for h in range(2):
            if t > 0:
                cw(t - 1, h).wait_recv()
            if t < far - 1 or h == 0:
                cw(t, h).start()
            if t > 0:
                ccw(t - 1, h).wait_recv()
            if t < far - 1 or h == 1:
                ccw(t, h).start()

    def piece(d, q):
        source = ring_row(pos + ring - d)
        dest_col = lax.div(source, nr)
        target = row_at(z, y, lax.rem(core + q, 2))
        return (
            dest_col,
            lax.rem(source, nr),
            pltpu.make_async_remote_copy(
                src_ref=mst.at[d, q],
                dst_ref=accb.at[c, lax.rem(source, nr)],
                send_sem=m_send.at[d, q],
                recv_sem=m_recv.at[c, lax.rem(source, nr)],
                device_id=(target, dest_col),
                device_id_type=MESH,
            ),
        )

    def triangle(blocks):
        for q in (1, 0):
            who = lax.rem(core + q, 2)

            def step(s, acc):
                acc = list(acc)
                for k in range(I):
                    rv = [rbuf[d, pl.ds(pl.multiple_of((s * I + k) * I, I), I), :] for d in blocks]
                    for i in range(I):
                        lv = lall[who, pl.ds(s * 64 + i * I + k, 1), :]
                        for n in range(len(blocks)):
                            acc[n * I + i] = acc[n * I + i] + lv * rv[n]
                return tuple(acc)

            acc = lax.fori_loop(
                0, nr, step, tuple(jnp.zeros((I, channels), f32) for _ in range(I * len(blocks)))
            )
            for n, d in enumerate(blocks):
                for i in range(I):
                    mst[d, q, i * I : (i + 1) * I, :] = acc[n * I + i]
                dest_col, slot, copy = piece(d, q)
                if q == 1:
                    copy.start()
                else:

                    @pl.when(dest_col == c)
                    def _():
                        accb[c, slot] = mst[d, q]

                    @pl.when(dest_col != c)
                    def _():
                        copy.start()

    forward(0)
    l_copy.start()
    l_copy.wait_recv()
    triangle([0])
    for t in range(1, far):
        forward(t)
        triangle([t, ring - t])
    cw(far - 1, 0).wait_recv()
    ccw(far - 1, 1).wait_recv()
    triangle([far])

    for s in range(nr):
        for k in range(C):
            mine = jnp.logical_and(c == k, core == s % 2)

            @pl.when(jnp.logical_not(mine))
            def _():
                pltpu.make_async_remote_copy(
                    src_ref=mst.at[0, 0],
                    dst_ref=accb.at[k, s],
                    send_sem=m_send.at[0, 0],
                    recv_sem=m_recv.at[k, s],
                    device_id=(core_row, c),
                    device_id_type=MESH,
                ).wait_recv()

    out_h, out_l = split(tri_out_ref[...])
    out_hh = jnp.concatenate([out_h, out_h], 0)
    for n in range(nr // chunk_slots):
        sl = pl.ds(n * chunk, chunk)
        mixed = accb[0, n * chunk_slots : (n + 1) * chunk_slots].reshape(chunk, channels)
        for k in range(1, C):
            mixed = mixed + accb[k, n * chunk_slots : (n + 1) * chunk_slots].reshape(chunk, channels)
        nh, nl = split(layer_norm(mixed))
        t = dot_nn(jnp.concatenate([nh, nl], 1), out_hh) + dot_nn(nh, out_l)
        t = pm_ref[sl, :] + gate_ref[sl, :] * t
        for s in range(chunk_slots):
            for i in range(I):
                at = i * J + (n * chunk_slots + s) * I
                out_ref[at : at + I, :] = t[(s * I + i) * I : (s * I + i + 1) * I]

    for t in range(zs):
        slot, source, goes_up, goes_down = a_links(t)

        @pl.when(goes_up)
        def _():
            a_copy(slot, a_up.at[t], up_row).wait_send()

        @pl.when(goes_down)
        def _():
            a_copy(slot, a_down.at[t], down_row).wait_send()

        a_copy(slot, a_y.at[t], y_row).wait_send()
        a_copy(slot, a_core.at[t, 0], core_row).wait_send()
        a_copy(near(t) * 4 + (1 - y) * 2 + core, a_core.at[t, 1], core_row).wait_send()
    l_copy.wait_send()
    for t in range(far):
        for h in range(2):
            if t < far - 1 or h == 0:
                cw(t, h).wait_send()
            if t < far - 1 or h == 1:
                ccw(t, h).wait_send()
    for d in range(ring):
        dest_col, _, copy = piece(d, 0)

        @pl.when(dest_col != c)
        def _():
            copy.wait_send()

        piece(d, 1)[2].wait_send()


def per_device(R, C, msa, pair, first, second, outer_w, tri_in, gate_w, tri_out):
    S, I, depth = msa.shape
    J, channels = pair.shape[1:]
    half = first.shape[1]
    nr = R // C
    zs = nr // 4
    ring = R // 2
    rows = nr * I * I
    dma = pltpu.SemaphoreType.DMA
    out = pl.pallas_call(
        functools.partial(kernel, (S, I, J, R, C, half, channels)),
        out_shape=jax.ShapeDtypeStruct((I * J, channels), f32),
        in_specs=[pl.BlockSpec(memory_space=pltpu.VMEM)] * 8,
        out_specs=pl.BlockSpec(memory_space=pltpu.VMEM),
        scratch_shapes=[
            pltpu.VMEM((depth // 128, S * I, 128), f32),
            pltpu.VMEM((I * half, S), f32),
            pltpu.VMEM((I * half, S), f32),
            pltpu.VMEM((nr, half * I, S), f32),
            pltpu.VMEM((half * half, channels), f32),
            pltpu.VMEM((nr, I * I, half * half), f32),
            pltpu.VMEM((rows, channels), f32),
            pltpu.VMEM((rows, channels), f32),
            pltpu.VMEM((rows, channels), f32),
            pltpu.VMEM((2, rows, channels), f32),
            pltpu.VMEM((ring, rows, channels), f32),
            pltpu.VMEM((ring, 2, I * I, channels), f32),
            pltpu.VMEM((C, nr, I * I, channels), f32),
            dma((zs,)),
            dma((zs,)),
            dma((zs,)),
            dma((zs, 2)),
            dma((nr,)),
            dma((2,)),
            dma((ring // 2, 2)),
            dma((ring // 2, 2)),
            dma((ring, 2)),
            dma((ring, 2)),
            dma((C, nr)),
        ],
        compiler_params=pltpu.CompilerParams(
            collective_id=0, has_side_effects=True, vmem_limit_bytes=48 * 1024 * 1024
        ),
        cost_estimate=pl.CostEstimate(
            flops=6 * 180 * 10**6, bytes_accessed=3 * 10**6, transcendentals=200000
        ),
    )(
        msa.reshape(S * I, depth),
        pair.reshape(I * J, channels),
        first,
        second,
        outer_w,
        tri_in,
        gate_w,
        tri_out,
    )
    return out.reshape(I, J, channels)


def solution(mesh):
    placed = (P(None, "row", None), P("row", "col", None), P(), P(), P(), P(), P(), P())
    return jax.shard_map(
        functools.partial(per_device, mesh.shape["row"], mesh.shape["col"]),
        mesh=mesh,
        in_specs=placed,
        out_specs=P("row", "col", None),
        check_vma=False,
    )
```

time: 255 us -> 57.2 us (0.22)
  waiting for transfers between devices: 145 us -> 0 us
  Pallas kernels: 0 us -> 49.9 us
  matrix products: 43.3 us -> 0 us
  local copies, waits for them, and re-layouts: 27.7 us -> 6.55 us
  blocking collectives: 16.1 us -> 0 us
  between operations: 13.6 us -> 0.04 us
  other arithmetic: 5.98 us -> 0 us
    psum x1 -> x0, waiting for transfers between devices: 103 us -> none  [broadcast(): return lax.psum(kept, axis)]
    pallas_call x0 -> x1, Pallas kernels: none -> 49.9 us  [per_device(): pl.pallas_call(functools.partial(kernel, (S, I, J, R, C, half, channels))...]
    dot_general x15 -> x0, matrix products: 43.3 us -> none  [the longest x8 16.2 us: per_device(): jnp.einsum('ikc,jkc->ijc', full_left, panel_rows, precision=top_precision)]
    all_gather x1 -> x0, waiting for transfers between devices: 41.9 us -> none  [per_device(): lax.all_gather(right_alignment_proj, 'row', axis=1, tiled=True)]
    all_gather x2 -> x0, blocking collectives: 16.1 us -> none  [the longest x1 8.33 us: per_device(): lax.all_gather(right_edge, 'col', axis=1, tiled=True)]
    psum x8 -> x0, local copies, waits for them, and re-layouts: 14 us -> none  [broadcast(): return lax.psum(kept, axis)]
    div x1 -> x0, local copies, waits for them, and re-layouts: 8.76 us -> none  [per_device(): jnp.einsum('emp,eqk->mqpk', left_alignment_proj, right_factor_columns, pr...]
    unnamed x14 -> x15, local copies, waits for them, and re-layouts: 0.03 us -> 6.55 us
  transfers between devices with their start and end apart: 2 -> 0, of which waited for: 2 -> 0; matrix products, arithmetic and copies ran while one was open for 1% -> 0% of each run, Pallas kernels for 0% -> 0%
where the time goes in v1:
time: 57.2 us; the launch traced here: 56.5 us
  Pallas kernels  49.9 us (87%)
  local copies, waits for them, and re-layouts  6.55 us (11%)
    pallas_call x1, Pallas kernels, per_device(): pl.pallas_call(functools.partial(kernel, (S, I, J, R, C, half, channels))...  49.9 us
    unnamed x15, local copies, waits for them, and re-layouts  6.55 us

profile of v1, /device:TPU:3, one launch (start us, length us, event | category | flops | bytes accessed | tf_op | source)
XLA Modules:
  0.0 56.5 jit_solution(10341984833380071879)
XLA Ops:
  0.0 0.0 copy-start.2
  0.0 0.9 %copy.9.first_ref = f32[256,32]{1,0:T(8,128)S(1)} copy(f32[256,32]{0,1:T(8,128)} %param.10) | data formatting | bytes 65536 | tf_op args[2]
  0.9 0.0 copy-start.4
  0.9 0.9 %copy.10.second_ref = f32[256,32]{1,0:T(8,128)S(1)} copy(f32[256,32]{0,1:T(8,128)} %param.11) | data formatting | bytes 65536 | tf_op args[3]
  1.8 0.0 copy-done.2
  1.8 0.0 copy-done.4
  1.8 0.0 copy-start
  1.8 1.2 %copy-done = f32[128,8,256]{2,1,0:T(8,128)S(1)} copy-done((f32[128,8,256]{2,1,0:T(8,128)S(1)}, f32[128,8,256]{2,1,0:T(8,128)}, u32[]{:S(2)}) %copy-start) | copy-done | bytes 1048600
  3.0 0.0 copy-start.1
  3.0 1.0 %copy-done.1 = f32[1024,128]{1,0:T(8,128)S(1)} copy-done((f32[1024,128]{1,0:T(8,128)S(1)}, f32[1024,128]{1,0:T(8,128)}, u32[]{:S(2)}) %copy-start.1) | copy-done | bytes 524312
  4.1 0.0 copy-start.3
  4.1 0.9 %copy-done.3 = f32[128,512]{1,0:T(8,128)S(1)} copy-done((f32[128,512]{1,0:T(8,128)S(1)}, f32[128,512]{1,0:T(8,128)}, u32[]{:S(2)}) %copy-start.3) | copy-done | bytes 262168
  5.0 0.0 copy-start.5
  5.0 0.8 %copy-done.5 = f32[128,128]{1,0:T(8,128)S(1)} copy-done((f32[128,128]{1,0:T(8,128)S(1)}, f32[128,128]{1,0:T(8,128)}, u32[]{:S(2)}) %copy-start.5) | copy-done | bytes 65560
  5.9 49.9 %shard_map.82 = f32[512,128]{1,0:T(8,128)S(1)} custom-call(f32[1024,256]{1,0:T(8,128)S(1)} %bitcast.4, f32[512,128]{1,0:T(8,128)S(1)} %bitcast.5, f32[256,32]{1,0:T(8,128)S(1)} %copy.9.first_ref, f32[256,32]{1,0:T(8,128)S(1)} %copy.10.second_ref, f32[1024,128]{1,0:T(8,128)S(1)} %copy-done.1, f32[128,512]{1,0:T(8,128)S(1)} %copy-done.3, ...), custom_call_target="tpu_custom_call" | custom-call | flops 1080000000 | bytes 3000000 | tf_op jit(solution)/shard_map/pallas_call | solution.py:434
  55.8 0.7 %copy.12 = f32[8,64,128]{2,1,0:T(8,128)} copy(f32[8,64,128]{2,1,0:T(8,128)S(1)} %bitcast.3) | data formatting | bytes 524288
Async XLA Ops:
  0.0 1.8 %copy-start.2 = (f32[8,64,128]{2,1,0:T(8,128)S(1)}, f32[8,64,128]{2,1,0:T(8,128)}, u32[]{:S(2)}) copy-start(f32[8,64,128]{2,1,0:T(8,128)} %param.9) | copy-start | bytes 786436
  0.9 0.9 %copy-start.4 = (f32[128,128]{1,0:T(8,128)S(1)}, f32[128,128]{1,0:T(8,128)}, u32[]{:S(2)}) copy-start(f32[128,128]{1,0:T(8,128)} %gate_w_ref.1) | copy-start | bytes 196612
  1.8 1.2 %copy-start = (f32[128,8,256]{2,1,0:T(8,128)S(1)}, f32[128,8,256]{2,1,0:T(8,128)}, u32[]{:S(2)}) copy-start(f32[128,8,256]{2,1,0:T(8,128)} %param.8) | copy-start | bytes 3145732
  3.0 1.0 %copy-start.1 = (f32[1024,128]{1,0:T(8,128)S(1)}, f32[1024,128]{1,0:T(8,128)}, u32[]{:S(2)}) copy-start(f32[1024,128]{1,0:T(8,128)} %outer_ref.1) | copy-start | bytes 1572868
  4.1 0.9 %copy-start.3 = (f32[128,512]{1,0:T(8,128)S(1)}, f32[128,512]{1,0:T(8,128)}, u32[]{:S(2)}) copy-start(f32[128,512]{1,0:T(8,128)} %tri_in_ref.1) | copy-start | bytes 786436
  5.0 0.8 %copy-start.5 = (f32[128,128]{1,0:T(8,128)S(1)}, f32[128,128]{1,0:T(8,128)}, u32[]{:S(2)}) copy-start(f32[128,128]{1,0:T(8,128)} %tri_out_ref.1) | copy-start | bytes 196612

commit v2 on v1

--- a/solution.py
+++ b/solution.py
@@ -11,6 +11,7 @@
 MESH = pl.DeviceIdType.MESH
 f32 = jnp.float32
 bf16 = jnp.bfloat16
+pieces = 4
 
 
 def split(x):
@@ -40,6 +41,15 @@
 
 def kernel(
     dims,
+    msa_hbm,
+    pair_hbm,
+    first_hbm,
+    second_hbm,
+    outer_hbm,
+    tri_in_hbm,
+    gate_w_hbm,
+    tri_out_hbm,
+    out_ref,
     msa_ref,
     pair_ref,
     first_ref,
@@ -48,7 +58,6 @@
     tri_in_ref,
     gate_w_ref,
     tri_out_ref,
-    out_ref,
     nm_ref,
     lt_ref,
     rt_ref,
@@ -67,6 +76,7 @@
     a_y,
     a_core,
     a_recv,
+    in_sem,
     l_sem,
     ring_cw,
     ring_ccw,
@@ -80,6 +90,7 @@
     zs = nr // 4
     ring = R // 2
     rows = nr * 64
+    parts = max(2, zs)
 
     r = lax.axis_index("row")
     c = lax.axis_index("col")
@@ -101,6 +112,24 @@
     down_row = row_at(lax.rem(z + Z - 1, Z), y, core)
     y_row = row_at(z, 1 - y, core)
     core_row = row_at(z, y, 1 - core)
+
+    loads = [
+        pltpu.make_async_copy(src, dst, in_sem.at[n])
+        for n, (src, dst) in enumerate(
+            (
+                (msa_hbm, msa_ref),
+                (first_hbm, first_ref),
+                (second_hbm, second_ref),
+                (outer_hbm, outer_ref),
+                (pair_hbm, pair_ref),
+                (tri_in_hbm, tri_in_ref),
+                (gate_w_hbm, gate_w_ref),
+                (tri_out_hbm, tri_out_ref),
+            )
+        )
+    ]
+    for load in loads:
+        load.start()
 
     barrier = pltpu.get_barrier_semaphore()
     greet = [(up_row, c), (down_row, c), (y_row, c), (core_row, c)]
@@ -110,10 +139,10 @@
     for target in greet:
         pl.semaphore_signal(barrier, inc=1, device_id=target, device_id_type=MESH)
 
-    both = jnp.concatenate(
-        [first_ref[...], second_ref[...], jnp.zeros((first_ref.shape[0], 128 - 2 * half), f32)], 1
-    ).T
-    both_h, both_l = split(both[: 2 * half])
+    for load in loads[:3]:
+        load.wait()
+    both = jnp.concatenate([first_ref[...], second_ref[...]], 0)
+    both_h, both_l = split(both)
     both_hl = jnp.concatenate([both_h, both_l], 0)
     depth = msa_ref.shape[1]
     normed = layer_norm(msa_ref[...])
@@ -136,23 +165,25 @@
 
     pl.semaphore_wait(barrier, len(greet))
 
-    def a_copy(slot, send, target):
+    piece_rows = half * I // pieces
+
+    def a_copy(slot, u, send, target):
+        at = rg.at[slot, pl.ds(u * piece_rows, piece_rows)]
         return pltpu.make_async_remote_copy(
-            src_ref=rg.at[slot],
-            dst_ref=rg.at[slot],
+            src_ref=at,
+            dst_ref=at,
             send_sem=send,
-            recv_sem=a_recv.at[slot],
+            recv_sem=a_recv.at[slot, u],
             device_id=(target, c),
             device_id_type=MESH,
         )
 
-    flip = (z > c * zs).astype(jnp.int32)
-
-    def near(t):
+    def turned(t, zz):
+        flip = (zz > c * zs).astype(jnp.int32)
         return t + flip * (zs - 1 - 2 * t)
 
     def a_links(t):
-        zi = near(t)
+        zi = turned(t, z)
         source = c * zs + zi
         slot = zi * 4 + y * 2 + core
         return (
@@ -162,24 +193,34 @@
             jnp.logical_and(z <= source, z > 0),
         )
 
-    for t in range(zs):
+    def a_line(t):
         slot, source, goes_up, goes_down = a_links(t)
-
-        @pl.when(z != source)
-        def _():
-            a_copy(slot, a_y.at[t], y_row).wait_recv()
-
-        @pl.when(goes_up)
-        def _():
-            a_copy(slot, a_up.at[t], up_row).start()
-
-        @pl.when(goes_down)
-        def _():
-            a_copy(slot, a_down.at[t], down_row).start()
-
-        a_copy(slot, a_y.at[t], y_row).start()
-        a_copy(slot, a_core.at[t, 0], core_row).start()
-
+        for u in range(pieces):
+
+            @pl.when(z != source)
+            def _():
+                a_copy(slot, u, a_y.at[t, u], y_row).wait_recv()
+
+            @pl.when(goes_up)
+            def _():
+                a_copy(slot, u, a_up.at[t, u], up_row).start()
+
+            @pl.when(goes_down)
+            def _():
+                a_copy(slot, u, a_down.at[t, u], down_row).start()
+
+            a_copy(slot, u, a_y.at[t, u], y_row).start()
+            a_copy(slot, u, a_core.at[t, 0, u], core_row).start()
+
+    def a_across(t):
+        slot = turned(t, z) * 4 + (1 - y) * 2 + core
+        for u in range(pieces):
+            a_copy(slot, u, a_core.at[t, 1, u], core_row).wait_recv()
+            a_copy(slot, u, a_core.at[t, 1, u], core_row).start()
+
+    a_line(0)
+
+    loads[3].wait()
     for b in range(half):
         wp_ref[b * half : (b + 1) * half, :] = outer_ref[pl.ds(b, half, stride=half), :]
 
@@ -209,96 +250,106 @@
                 for g in range(half // 4):
                     x_ref[slot, i * I : (i + 1) * I, g * 128 : (g + 1) * 128] = v[q][g]
 
-    for t in range(zs):
-        slot = a_links(t)[0]
-        outer_block(slot)
-    for t in range(zs):
-        slot = near(t) * 4 + (1 - y) * 2 + core
-        a_copy(slot, a_core.at[t, 1], core_row).wait_recv()
-        a_copy(slot, a_core.at[t, 1], core_row).start()
-    for t in range(zs):
-        outer_block(near(t) * 4 + (1 - y) * 2 + core)
-    for yy in range(2):
-        for t in range(zs):
-            slot = near(t) * 4 + lax.rem(y + yy, 2) * 2 + 1 - core
-            a_copy(slot, a_core.at[t, 1], core_row).wait_recv()
-            outer_block(slot)
-
     wh, wl = split(wp_ref[...])
     w_hl = jnp.concatenate([wh, wl], 1)
+    for load in loads[4:]:
+        load.wait()
     in_w = jnp.concatenate([tri_in_ref[...], gate_w_ref[...]], 1)
     in_h, in_l = split(in_w)
     in_hh = jnp.concatenate([in_h, in_h], 0)
-    chunk_slots = min(4, nr)
-    chunk = chunk_slots * 64
-    for n in range(nr // chunk_slots):
-        xh, xl = split(x_ref[n * chunk_slots : (n + 1) * chunk_slots].reshape(chunk, half * half))
+    out_h, out_l = split(tri_out_ref[...])
+    out_hh = jnp.concatenate([out_h, out_h], 0)
+    ch = tri_out_ref.shape[0]
+    group = 4 * 64
+
+    def pair_group(zi):
+        xh, xl = split(x_ref[pl.ds(zi * 4, 4)].reshape(group, half * half))
         t = dot_nn(xh, w_hl)
         t = t[:, :channels] + t[:, channels:] + dot_nn(xl, wh)
         own = jnp.concatenate(
             [
-                pair_ref[i * J + s * I : i * J + (s + 1) * I, :]
-                for s in range(n * chunk_slots, (n + 1) * chunk_slots)
+                pair_ref[pl.ds(pl.multiple_of(i * J + (zi * 4 + s) * I, I), I), :]
+                for s in range(4)
                 for i in range(I)
             ],
             0,
         )
         mid = own + t
-        sl = pl.ds(n * chunk, chunk)
+        sl = pl.ds(pl.multiple_of(zi * group, group), group)
         pm_ref[sl, :] = mid
         nh, nl = split(layer_norm(mid))
         pr = dot_nn(jnp.concatenate([nh, nl], 1), in_hh) + dot_nn(nh, in_l)
-        ch = tri_out_ref.shape[0]
+        redge_ref[sl, :] = sigmoid(pr[:, 3 * ch : 4 * ch]) * pr[:, 2 * ch : 3 * ch]
+        for s in range(4):
+            for k in range(I):
+                at = pl.multiple_of(zi * group + (s * I + k) * I, I)
+                rbuf[0, pl.ds(at, I), :] = redge_ref[
+                    pl.ds(zi * group + s * 64 + k, I, stride=I), :
+                ]
+        for n in range(parts // zs):
+            h = zi * (parts // zs) + n
+            cw(0, h).start()
+            ccw(0, h).start()
         lall[core, sl, :] = sigmoid(pr[:, ch : 2 * ch]) * pr[:, :ch]
-        redge_ref[sl, :] = sigmoid(pr[:, 3 * ch : 4 * ch]) * pr[:, 2 * ch : 3 * ch]
+        l_copy(zi).start()
         gate_ref[sl, :] = sigmoid(pr[:, 4 * ch :])
 
-    for s in range(nr):
-        for k in range(I):
-            at = (s * I + k) * I
-            rbuf[0, at : at + I, :] = redge_ref[pl.ds(s * 64 + k, I, stride=I), :]
-
-    part = rows // 2
+    part = rows // parts
+    next_row = ring_row(pos + 1)
+    prev_row = ring_row(pos + ring - 1)
+    far = ring // 2
 
     def ring_copy(src, dst, h, send, target):
+        at = pl.ds(pl.multiple_of(h * part, part), part)
         return pltpu.make_async_remote_copy(
-            src_ref=rbuf.at[src, pl.ds(h * part, part)],
-            dst_ref=rbuf.at[dst, pl.ds(h * part, part)],
+            src_ref=rbuf.at[src, at],
+            dst_ref=rbuf.at[dst, at],
             send_sem=send,
             recv_sem=ring_recv.at[dst, h],
             device_id=(target, c),
             device_id_type=MESH,
         )
 
-    next_row = ring_row(pos + 1)
-    prev_row = ring_row(pos + ring - 1)
-    far = ring // 2
-
     def cw(t, h):
         return ring_copy(t, t + 1, h, ring_cw.at[t, h], next_row)
 
     def ccw(t, h):
         return ring_copy((ring - t) % ring, ring - t - 1, h, ring_ccw.at[t, h], prev_row)
 
-    l_copy = pltpu.make_async_remote_copy(
-        src_ref=lall.at[core],
-        dst_ref=lall.at[core],
-        send_sem=l_sem.at[0],
-        recv_sem=l_sem.at[1],
-        device_id=(core_row, c),
-        device_id_type=MESH,
-    )
+    def l_copy(zi):
+        at = lall.at[core, pl.ds(pl.multiple_of(zi * group, group), group)]
+        return pltpu.make_async_remote_copy(
+            src_ref=at,
+            dst_ref=at,
+            send_sem=l_sem.at[0, zi],
+            recv_sem=l_sem.at[1, zi],
+            device_id=(core_row, c),
+            device_id_type=MESH,
+        )
+
+    def block_order(d, h):
+        if zs == 1:
+            return h
+        return turned(h, lax.div(ring_row(pos + ring - d), 4))
 
     def forward(t):
-        for h in range(2):
-            if t > 0:
+        if t == far - 1:
+            for h in range(parts // 2):
                 cw(t - 1, h).wait_recv()
-            if t < far - 1 or h == 0:
                 cw(t, h).start()
-            if t > 0:
+                ccw(t - 1, parts // 2 + h).wait_recv()
+                ccw(t, parts // 2 + h).start()
+            for h in range(parts // 2):
+                cw(t - 1, parts // 2 + h).wait_recv()
                 ccw(t - 1, h).wait_recv()
-            if t < far - 1 or h == 1:
-                ccw(t, h).start()
+            return
+        for n in range(parts):
+            h = block_order(t, n)
+            cw(t - 1, h).wait_recv()
+            cw(t, h).start()
+            h = block_order(ring - t, n)
+            ccw(t - 1, h).wait_recv()
+            ccw(t, h).start()
 
     def piece(d, q):
         source = ring_row(pos + ring - d)
@@ -350,23 +401,14 @@
                     def _():
                         copy.start()
 
-    forward(0)
-    l_copy.start()
-    l_copy.wait_recv()
-    triangle([0])
-    for t in range(1, far):
-        forward(t)
-        triangle([t, ring - t])
-    cw(far - 1, 0).wait_recv()
-    ccw(far - 1, 1).wait_recv()
-    triangle([far])
-
-    for s in range(nr):
-        for k in range(C):
-            mine = jnp.logical_and(c == k, core == s % 2)
-
-            @pl.when(jnp.logical_not(mine))
-            def _():
+    def finish(d):
+        source = ring_row(pos + ring - d) - core
+
+        @pl.when(lax.div(source, nr) == c)
+        def _():
+            base = lax.rem(source, nr)
+
+            def arrived(k, s):
                 pltpu.make_async_remote_copy(
                     src_ref=mst.at[0, 0],
                     dst_ref=accb.at[k, s],
@@ -376,41 +418,81 @@
                     device_id_type=MESH,
                 ).wait_recv()
 
-    out_h, out_l = split(tri_out_ref[...])
-    out_hh = jnp.concatenate([out_h, out_h], 0)
-    for n in range(nr // chunk_slots):
-        sl = pl.ds(n * chunk, chunk)
-        mixed = accb[0, n * chunk_slots : (n + 1) * chunk_slots].reshape(chunk, channels)
-        for k in range(1, C):
-            mixed = mixed + accb[k, n * chunk_slots : (n + 1) * chunk_slots].reshape(chunk, channels)
-        nh, nl = split(layer_norm(mixed))
-        t = dot_nn(jnp.concatenate([nh, nl], 1), out_hh) + dot_nn(nh, out_l)
-        t = pm_ref[sl, :] + gate_ref[sl, :] * t
-        for s in range(chunk_slots):
-            for i in range(I):
-                at = i * J + (n * chunk_slots + s) * I
-                out_ref[at : at + I, :] = t[(s * I + i) * I : (s * I + i + 1) * I]
+            arrived(c, base + 1 - core)
+            for n in range(1, C):
+                k = lax.rem(c + n, C)
+                arrived(k, base)
+                arrived(k, base + 1)
+            mixed = accb[0, pl.ds(base, 2)].reshape(128, channels)
+            for k in range(1, C):
+                mixed = mixed + accb[k, pl.ds(base, 2)].reshape(128, channels)
+            nh, nl = split(layer_norm(mixed))
+            t = dot_nn(jnp.concatenate([nh, nl], 1), out_hh) + dot_nn(nh, out_l)
+            sl = pl.ds(pl.multiple_of(base * 64, 64), 128)
+            t = pm_ref[sl, :] + gate_ref[sl, :] * t
+            for s in range(2):
+                for i in range(I):
+                    at = pl.multiple_of(i * J + (base + s) * I, I)
+                    out_ref[pl.ds(at, I), :] = t[(s * I + i) * I : (s * I + i + 1) * I]
+
+    outer_block(a_links(0)[0])
+    for t in range(1, zs):
+        a_line(t)
+    a_across(0)
+    for t in range(zs):
+        zi = turned(t, z)
+        if t > 0:
+            outer_block(zi * 4 + y * 2 + core)
+        outer_block(zi * 4 + (1 - y) * 2 + core)
+        for yy in (y, 1 - y):
+            slot = zi * 4 + yy * 2 + 1 - core
+            for u in range(pieces):
+                a_copy(slot, u, a_core.at[t, 1, u], core_row).wait_recv()
+            outer_block(slot)
+        if t + 1 < zs:
+            a_across(t + 1)
+        pair_group(zi)
+
+    for t in range(zs):
+        l_copy(t).wait_recv()
+    pending = [0]
+    triangle([0])
+    for t in range(1, far):
+        forward(t)
+        triangle([t, ring - t])
+        for d in pending:
+            finish(d)
+        pending = [t, ring - t]
+    for d in pending:
+        finish(d)
+    for h in range(parts // 2):
+        cw(far - 1, h).wait_recv()
+        ccw(far - 1, parts // 2 + h).wait_recv()
+    triangle([far])
+    finish(far)
 
     for t in range(zs):
         slot, source, goes_up, goes_down = a_links(t)
-
-        @pl.when(goes_up)
-        def _():
-            a_copy(slot, a_up.at[t], up_row).wait_send()
-
-        @pl.when(goes_down)
-        def _():
-            a_copy(slot, a_down.at[t], down_row).wait_send()
-
-        a_copy(slot, a_y.at[t], y_row).wait_send()
-        a_copy(slot, a_core.at[t, 0], core_row).wait_send()
-        a_copy(near(t) * 4 + (1 - y) * 2 + core, a_core.at[t, 1], core_row).wait_send()
-    l_copy.wait_send()
+        across = turned(t, z) * 4 + (1 - y) * 2 + core
+        for u in range(pieces):
+
+            @pl.when(goes_up)
+            def _():
+                a_copy(slot, u, a_up.at[t, u], up_row).wait_send()
+
+            @pl.when(goes_down)
+            def _():
+                a_copy(slot, u, a_down.at[t, u], down_row).wait_send()
+
+            a_copy(slot, u, a_y.at[t, u], y_row).wait_send()
+            a_copy(slot, u, a_core.at[t, 0, u], core_row).wait_send()
+            a_copy(across, u, a_core.at[t, 1, u], core_row).wait_send()
+        l_copy(t).wait_send()
     for t in range(far):
-        for h in range(2):
-            if t < far - 1 or h == 0:
+        for h in range(parts):
+            if t < far - 1 or h < parts // 2:
                 cw(t, h).wait_send()
-            if t < far - 1 or h == 1:
+            if t < far - 1 or h >= parts // 2:
                 ccw(t, h).wait_send()
     for d in range(ring):
         dest_col, _, copy = piece(d, 0)
@@ -430,13 +512,25 @@
     zs = nr // 4
     ring = R // 2
     rows = nr * I * I
+    parts = max(2, zs)
+    operands = (
+        msa.reshape(S * I, depth),
+        pair.reshape(I * J, channels),
+        first.T,
+        second.T,
+        outer_w,
+        tri_in,
+        gate_w,
+        tri_out,
+    )
     dma = pltpu.SemaphoreType.DMA
     out = pl.pallas_call(
         functools.partial(kernel, (S, I, J, R, C, half, channels)),
         out_shape=jax.ShapeDtypeStruct((I * J, channels), f32),
-        in_specs=[pl.BlockSpec(memory_space=pltpu.VMEM)] * 8,
+        in_specs=[pl.BlockSpec(memory_space=pltpu.HBM)] * 8,
         out_specs=pl.BlockSpec(memory_space=pltpu.VMEM),
-        scratch_shapes=[
+        scratch_shapes=[pltpu.VMEM(x.shape, f32) for x in operands]
+        + [
             pltpu.VMEM((depth // 128, S * I, 128), f32),
             pltpu.VMEM((I * half, S), f32),
             pltpu.VMEM((I * half, S), f32),
@@ -450,34 +544,26 @@
             pltpu.VMEM((ring, rows, channels), f32),
             pltpu.VMEM((ring, 2, I * I, channels), f32),
             pltpu.VMEM((C, nr, I * I, channels), f32),
-            dma((zs,)),
-            dma((zs,)),
-            dma((zs,)),
-            dma((zs, 2)),
-            dma((nr,)),
-            dma((2,)),
-            dma((ring // 2, 2)),
-            dma((ring // 2, 2)),
-            dma((ring, 2)),
+            dma((zs, pieces)),
+            dma((zs, pieces)),
+            dma((zs, pieces)),
+            dma((zs, 2, pieces)),
+            dma((nr, pieces)),
+            dma((len(operands),)),
+            dma((2, zs)),
+            dma((ring // 2, parts)),
+            dma((ring // 2, parts)),
+            dma((ring, parts)),
             dma((ring, 2)),
             dma((C, nr)),
         ],
         compiler_params=pltpu.CompilerParams(
-            collective_id=0, has_side_effects=True, vmem_limit_bytes=48 * 1024 * 1024
+            collective_id=0, has_side_effects=True, vmem_limit_bytes=62 * 1024 * 1024
         ),
         cost_estimate=pl.CostEstimate(
             flops=6 * 180 * 10**6, bytes_accessed=3 * 10**6, transcendentals=200000
         ),
-    )(
-        msa.reshape(S * I, depth),
-        pair.reshape(I * J, channels),
-        first,
-        second,
-        outer_w,
-        tri_in,
-        gate_w,
-        tri_out,
-    )
+    )(*operands)
     return out.reshape(I, J, channels)
 
 

time: 57.2 us -> 48.4 us (0.85)
  the two profiles are of different devices: /device:TPU:3 before, /device:TPU:10 now
where the time goes in v2:
time: 48.4 us; the launch traced here: 48.2 us
  Pallas kernels  46.5 us (96%)
  local copies, waits for them, and re-layouts  1.67 us (3%)
    pallas_call x1, Pallas kernels, per_device(): pl.pallas_call(functools.partial(kernel, (S, I, J, R, C, half, channels))...  46.5 us
    unnamed x1, local copies, waits for them, and re-layouts  1.67 us

profile of v2, /device:TPU:10, one launch (start us, length us, event | category | flops | bytes accessed | tf_op | source)
XLA Modules:
  0.0 48.2 jit_solution(735753976669957720)
XLA Ops:
  0.0 46.5 %shard_map.82 = f32[512,128]{1,0:T(8,128)} custom-call(f32[1024,256]{1,0:T(8,128)} %bitcast.6, f32[512,128]{1,0:T(8,128)} %bitcast.7, f32[32,256]{1,0:T(8,128)} %bitcast.8, f32[32,256]{1,0:T(8,128)} %bitcast.9, f32[1024,128]{1,0:T(8,128)} %outer_hbm.1, f32[128,512]{1,0:T(8,128)} %tri_in_hbm.1, f32[128,128]{1,0:T(8,128)} %gate_w_hbm.1, f32[128,128]{1,0:T(8,128)} %tri_out_hbm.1), custom_call_target="tpu_custom_call" | custom-call | flops 1080000000 | bytes 3000000 | tf_op jit(solution)/shard_map/pallas_call | solution.py:527
  46.5 1.7 %copy.10 = f32[8,64,128]{2,1,0:T(8,128)} copy(f32[8,64,128]{2,1,0:T(8,128)} %bitcast.5) | data formatting | bytes 524288

commit v3 on v2

--- a/solution.py
+++ b/solution.py
@@ -77,10 +77,11 @@
     a_core,
     a_recv,
     in_sem,
-    l_sem,
-    ring_cw,
-    ring_ccw,
-    ring_recv,
+    l_send,
+    l_recv,
+    up_sem,
+    down_sem,
+    line_recv,
     m_send,
     m_recv,
 ):
@@ -88,7 +89,6 @@
     nr = R // C
     Z = R // 4
     zs = nr // 4
-    ring = R // 2
     rows = nr * 64
     parts = max(2, zs)
 
@@ -97,16 +97,8 @@
     core = lax.rem(r, 2)
     y = lax.rem(lax.div(r, 2), 2)
     z = lax.div(r, 4)
-    pos = z + y * (ring - 1 - 2 * z)
-
     def row_at(zz, yy, cc):
         return zz * 4 + yy * 2 + cc
-
-    def ring_row(q):
-        q = lax.rem(q, ring)
-        yy = lax.div(q, Z)
-        zz = q * (1 - yy) + (ring - 1 - q) * yy
-        return row_at(zz, yy, core)
 
     up_row = row_at(lax.rem(z + 1, Z), y, core)
     down_row = row_at(lax.rem(z + Z - 1, Z), y, core)
@@ -132,10 +124,11 @@
         load.start()
 
     barrier = pltpu.get_barrier_semaphore()
-    greet = [(up_row, c), (down_row, c), (y_row, c), (core_row, c)]
-    for d in range(1, C):
-        other = lax.rem(c + d, C)
-        greet += [(r, other), (core_row, other)]
+    greet = [(up_row, c), (down_row, c)]
+    for k in range(C):
+        for n in range(4):
+            if k or n:
+                greet.append((row_at(z, lax.rem(y + n // 2, 2), lax.rem(core + n, 2)), lax.rem(c + k, C)))
     for target in greet:
         pl.semaphore_signal(barrier, inc=1, device_id=target, device_id_type=MESH)
 
@@ -283,113 +276,120 @@
         for s in range(4):
             for k in range(I):
                 at = pl.multiple_of(zi * group + (s * I + k) * I, I)
-                rbuf[0, pl.ds(at, I), :] = redge_ref[
+                rbuf[z, pl.ds(at, I), :] = redge_ref[
                     pl.ds(zi * group + s * 64 + k, I, stride=I), :
                 ]
         for n in range(parts // zs):
-            h = zi * (parts // zs) + n
-            cw(0, h).start()
-            ccw(0, h).start()
-        lall[core, sl, :] = sigmoid(pr[:, ch : 2 * ch]) * pr[:, :ch]
-        l_copy(zi).start()
+            send_on(0, zi * (parts // zs) + n)
+        lall[2 * y + core, sl, :] = sigmoid(pr[:, ch : 2 * ch]) * pr[:, :ch]
+        l_copy(0, zi).start()
+        l_copy(1, zi).start()
         gate_ref[sl, :] = sigmoid(pr[:, 4 * ch :])
 
     part = rows // parts
-    next_row = ring_row(pos + 1)
-    prev_row = ring_row(pos + ring - 1)
-    far = ring // 2
-
-    def ring_copy(src, dst, h, send, target):
-        at = pl.ds(pl.multiple_of(h * part, part), part)
-        return pltpu.make_async_remote_copy(
-            src_ref=rbuf.at[src, at],
-            dst_ref=rbuf.at[dst, at],
-            send_sem=send,
-            recv_sem=ring_recv.at[dst, h],
-            device_id=(target, c),
-            device_id_type=MESH,
-        )
-
-    def cw(t, h):
-        return ring_copy(t, t + 1, h, ring_cw.at[t, h], next_row)
-
-    def ccw(t, h):
-        return ring_copy((ring - t) % ring, ring - t - 1, h, ring_ccw.at[t, h], prev_row)
-
-    def l_copy(zi):
-        at = lall.at[core, pl.ds(pl.multiple_of(zi * group, group), group)]
+
+    def line_copy(source, h, send, target):
+        at = rbuf.at[source, pl.ds(pl.multiple_of(h * part, part), part)]
         return pltpu.make_async_remote_copy(
             src_ref=at,
             dst_ref=at,
-            send_sem=l_sem.at[0, zi],
-            recv_sem=l_sem.at[1, zi],
+            send_sem=send,
+            recv_sem=line_recv.at[source, h],
+            device_id=(target, c),
+            device_id_type=MESH,
+        )
+
+    def line_up(t, h):
+        return line_copy(z - t, h, up_sem.at[t, h], up_row)
+
+    def line_down(t, h):
+        return line_copy(z + t, h, down_sem.at[t, h], down_row)
+
+    def send_on(t, h):
+        @pl.when(jnp.logical_and(z >= t, z < Z - 1))
+        def _():
+            line_up(t, h).start()
+
+        @pl.when(jnp.logical_and(z + t < Z, z > 0))
+        def _():
+            line_down(t, h).start()
+
+    own_l = 2 * y + core
+
+    def l_copy(n, zi):
+        slot = own_l if n < 2 else 2 * (1 - y) + core
+        at = lall.at[slot, pl.ds(pl.multiple_of(zi * group, group), group)]
+        return pltpu.make_async_remote_copy(
+            src_ref=at,
+            dst_ref=at,
+            send_sem=l_send.at[n, zi],
+            recv_sem=l_recv.at[slot, zi],
+            device_id=(y_row if n == 1 else core_row, c),
+            device_id_type=MESH,
+        )
+
+    def l_arrived(slot, zi):
+        at = lall.at[slot, pl.ds(pl.multiple_of(zi * group, group), group)]
+        pltpu.make_async_remote_copy(
+            src_ref=at,
+            dst_ref=at,
+            send_sem=l_send.at[0, zi],
+            recv_sem=l_recv.at[slot, zi],
             device_id=(core_row, c),
             device_id_type=MESH,
-        )
-
-    def block_order(d, h):
+        ).wait_recv()
+
+    def part_order(source, n):
         if zs == 1:
-            return h
-        return turned(h, lax.div(ring_row(pos + ring - d), 4))
-
-    def forward(t):
-        if t == far - 1:
-            for h in range(parts // 2):
-                cw(t - 1, h).wait_recv()
-                cw(t, h).start()
-                ccw(t - 1, parts // 2 + h).wait_recv()
-                ccw(t, parts // 2 + h).start()
-            for h in range(parts // 2):
-                cw(t - 1, parts // 2 + h).wait_recv()
-                ccw(t - 1, h).wait_recv()
-            return
-        for n in range(parts):
-            h = block_order(t, n)
-            cw(t - 1, h).wait_recv()
-            cw(t, h).start()
-            h = block_order(ring - t, n)
-            ccw(t - 1, h).wait_recv()
-            ccw(t, h).start()
-
-    def piece(d, q):
-        source = ring_row(pos + ring - d)
-        dest_col = lax.div(source, nr)
-        target = row_at(z, y, lax.rem(core + q, 2))
+            return n
+        return turned(n, source)
+
+    def piece(d, source, q):
+        dest_col = lax.div(source, zs)
+        slot = lax.rem(source, zs) * 4 + own_l
+        target = row_at(z, lax.rem(y + q // 2, 2), lax.rem(core + q, 2))
         return (
             dest_col,
-            lax.rem(source, nr),
+            slot,
             pltpu.make_async_remote_copy(
                 src_ref=mst.at[d, q],
-                dst_ref=accb.at[c, lax.rem(source, nr)],
+                dst_ref=accb.at[c, slot],
                 send_sem=m_send.at[d, q],
-                recv_sem=m_recv.at[c, lax.rem(source, nr)],
+                recv_sem=m_recv.at[c, slot],
                 device_id=(target, dest_col),
                 device_id_type=MESH,
             ),
         )
 
-    def triangle(blocks):
-        for q in (1, 0):
-            who = lax.rem(core + q, 2)
+    def triangle(d, source, h, first, last):
+        for pair in ((2, 3), (1, 0)):
+            who = [2 * lax.rem(y + q // 2, 2) + lax.rem(core + q, 2) for q in pair]
 
             def step(s, acc):
                 acc = list(acc)
+                s = h * (nr // parts) + s
                 for k in range(I):
-                    rv = [rbuf[d, pl.ds(pl.multiple_of((s * I + k) * I, I), I), :] for d in blocks]
-                    for i in range(I):
-                        lv = lall[who, pl.ds(s * 64 + i * I + k, 1), :]
-                        for n in range(len(blocks)):
-                            acc[n * I + i] = acc[n * I + i] + lv * rv[n]
+                    rv = rbuf[source, pl.ds(pl.multiple_of((s * I + k) * I, I), I), :]
+                    for n in range(2):
+                        for i in range(I):
+                            lv = lall[who[n], pl.ds(s * 64 + i * I + k, 1), :]
+                            acc[n * I + i] = acc[n * I + i] + lv * rv
                 return tuple(acc)
 
-            acc = lax.fori_loop(
-                0, nr, step, tuple(jnp.zeros((I, channels), f32) for _ in range(I * len(blocks)))
-            )
-            for n, d in enumerate(blocks):
+            if first:
+                acc = tuple(jnp.zeros((I, channels), f32) for _ in range(2 * I))
+            else:
+                acc = tuple(
+                    mst[d, q, i * I : (i + 1) * I, :] for q in pair for i in range(I)
+                )
+            acc = lax.fori_loop(0, nr // parts, step, acc)
+            for n, q in enumerate(pair):
                 for i in range(I):
                     mst[d, q, i * I : (i + 1) * I, :] = acc[n * I + i]
-                dest_col, slot, copy = piece(d, q)
-                if q == 1:
+                if not last:
+                    continue
+                dest_col, slot, copy = piece(d, source, q)
+                if q:
                     copy.start()
                 else:
 
@@ -401,12 +401,10 @@
                     def _():
                         copy.start()
 
-    def finish(d):
-        source = ring_row(pos + ring - d) - core
-
-        @pl.when(lax.div(source, nr) == c)
+    def finish(source, exists):
+        @pl.when(jnp.logical_and(exists, lax.div(source, zs) == c))
         def _():
-            base = lax.rem(source, nr)
+            base = lax.rem(source, zs) * 4
 
             def arrived(k, s):
                 pltpu.make_async_remote_copy(
@@ -418,22 +416,23 @@
                     device_id_type=MESH,
                 ).wait_recv()
 
-            arrived(c, base + 1 - core)
+            for n in range(1, 4):
+                arrived(c, base + 2 * lax.rem(y + n // 2, 2) + lax.rem(core + n, 2))
             for n in range(1, C):
-                k = lax.rem(c + n, C)
-                arrived(k, base)
-                arrived(k, base + 1)
-            mixed = accb[0, pl.ds(base, 2)].reshape(128, channels)
-            for k in range(1, C):
-                mixed = mixed + accb[k, pl.ds(base, 2)].reshape(128, channels)
-            nh, nl = split(layer_norm(mixed))
-            t = dot_nn(jnp.concatenate([nh, nl], 1), out_hh) + dot_nn(nh, out_l)
-            sl = pl.ds(pl.multiple_of(base * 64, 64), 128)
-            t = pm_ref[sl, :] + gate_ref[sl, :] * t
-            for s in range(2):
-                for i in range(I):
-                    at = pl.multiple_of(i * J + (base + s) * I, I)
-                    out_ref[pl.ds(at, I), :] = t[(s * I + i) * I : (s * I + i + 1) * I]
+                for s in range(4):
+                    arrived(lax.rem(c + n, C), base + s)
+            for s in range(0, 4, 2):
+                mixed = accb[0, pl.ds(base + s, 2)].reshape(128, channels)
+                for k in range(1, C):
+                    mixed = mixed + accb[k, pl.ds(base + s, 2)].reshape(128, channels)
+                nh, nl = split(layer_norm(mixed))
+                t = dot_nn(jnp.concatenate([nh, nl], 1), out_hh) + dot_nn(nh, out_l)
+                sl = pl.ds(pl.multiple_of((base + s) * 64, 64), 128)
+                t = pm_ref[sl, :] + gate_ref[sl, :] * t
+                for n in range(2):
+                    for i in range(I):
+                        at = pl.multiple_of(i * J + (base + s + n) * I, I)
+                        out_ref[pl.ds(at, I), :] = t[(n * I + i) * I : (n * I + i + 1) * I]
 
     outer_block(a_links(0)[0])
     for t in range(1, zs):
@@ -454,22 +453,51 @@
         pair_group(zi)
 
     for t in range(zs):
-        l_copy(t).wait_recv()
-    pending = [0]
-    triangle([0])
-    for t in range(1, far):
-        forward(t)
-        triangle([t, ring - t])
-        for d in pending:
-            finish(d)
-        pending = [t, ring - t]
-    for d in pending:
-        finish(d)
-    for h in range(parts // 2):
-        cw(far - 1, h).wait_recv()
-        ccw(far - 1, parts // 2 + h).wait_recv()
-    triangle([far])
-    finish(far)
+        zi = turned(t, z)
+        l_arrived(2 * (1 - y) + core, zi)
+        l_copy(2, zi).start()
+    for t in range(zs):
+        zi = turned(t, z)
+        l_arrived(2 * y + 1 - core, zi)
+        l_arrived(2 * (1 - y) + 1 - core, zi)
+    for n in range(parts):
+        triangle(0, z, part_order(z, n), n == 0, n == parts - 1)
+    for t in range(1, Z):
+        for n in range(parts):
+            below = part_order(z - t, n)
+            above = part_order(z + t, n)
+
+            @pl.when(z >= t)
+            def _():
+                line_up(t, below).wait_recv()
+
+                @pl.when(z < Z - 1)
+                def _():
+                    line_up(t, below).start()
+
+            @pl.when(z + t < Z)
+            def _():
+                line_down(t, above).wait_recv()
+
+                @pl.when(z > 0)
+                def _():
+                    line_down(t, above).start()
+
+            @pl.when(z >= t)
+            def _():
+                triangle(t, z - t, below, n == 0, n == parts - 1)
+
+            @pl.when(z + t < Z)
+            def _():
+                triangle(Z - 1 + t, z + t, above, n == 0, n == parts - 1)
+
+        if t == 1:
+            finish(z, z >= 0)
+        else:
+            finish(z - t + 1, z >= t - 1)
+            finish(z + t - 1, z + t - 1 < Z)
+    finish(z - Z + 1, z >= Z - 1)
+    finish(z + Z - 1, z < 1)
 
     for t in range(zs):
         slot, source, goes_up, goes_down = a_links(t)
@@ -487,21 +515,40 @@
             a_copy(slot, u, a_y.at[t, u], y_row).wait_send()
             a_copy(slot, u, a_core.at[t, 0, u], core_row).wait_send()
             a_copy(across, u, a_core.at[t, 1, u], core_row).wait_send()
-        l_copy(t).wait_send()
-    for t in range(far):
+        for n in range(3):
+            l_copy(n, t).wait_send()
+    for t in range(Z):
         for h in range(parts):
-            if t < far - 1 or h < parts // 2:
-                cw(t, h).wait_send()
-            if t < far - 1 or h >= parts // 2:
-                ccw(t, h).wait_send()
-    for d in range(ring):
-        dest_col, _, copy = piece(d, 0)
-
-        @pl.when(dest_col != c)
+
+            @pl.when(jnp.logical_and(z >= t, z < Z - 1))
+            def _():
+                line_up(t, h).wait_send()
+
+            @pl.when(jnp.logical_and(z + t < Z, z > 0))
+            def _():
+                line_down(t, h).wait_send()
+
+    def pieces_left(d, source):
+        for q in range(4):
+            dest_col, _, copy = piece(d, source, q)
+            if q:
+                copy.wait_send()
+            else:
+
+                @pl.when(dest_col != c)
+                def _():
+                    copy.wait_send()
+
+    pieces_left(0, z)
+    for t in range(1, Z):
+
+        @pl.when(z >= t)
         def _():
-            copy.wait_send()
-
-        piece(d, 1)[2].wait_send()
+            pieces_left(t, z - t)
+
+        @pl.when(z + t < Z)
+        def _():
+            pieces_left(Z - 1 + t, z + t)
 
 
 def per_device(R, C, msa, pair, first, second, outer_w, tri_in, gate_w, tri_out):
@@ -510,7 +557,7 @@
     half = first.shape[1]
     nr = R // C
     zs = nr // 4
-    ring = R // 2
+    Z = R // 4
     rows = nr * I * I
     parts = max(2, zs)
     operands = (
@@ -540,9 +587,9 @@
             pltpu.VMEM((rows, channels), f32),
             pltpu.VMEM((rows, channels), f32),
             pltpu.VMEM((rows, channels), f32),
-            pltpu.VMEM((2, rows, channels), f32),
-            pltpu.VMEM((ring, rows, channels), f32),
-            pltpu.VMEM((ring, 2, I * I, channels), f32),
+            pltpu.VMEM((4, rows, channels), f32),
+            pltpu.VMEM((Z, rows, channels), f32),
+            pltpu.VMEM((2 * Z - 1, 4, I * I, channels), f32),
             pltpu.VMEM((C, nr, I * I, channels), f32),
             dma((zs, pieces)),
             dma((zs, pieces)),
@@ -550,11 +597,12 @@
             dma((zs, 2, pieces)),
             dma((nr, pieces)),
             dma((len(operands),)),
-            dma((2, zs)),
-            dma((ring // 2, parts)),
-            dma((ring // 2, parts)),
-            dma((ring, parts)),
-            dma((ring, 2)),
+            dma((3, zs)),
+            dma((4, zs)),
+            dma((Z, parts)),
+            dma((Z, parts)),
+            dma((Z, parts)),
+            dma((2 * Z - 1, 4)),
             dma((C, nr)),
         ],
         compiler_params=pltpu.CompilerParams(

time: 48.4 us -> 46.6 us (0.963)
  the two profiles are of different devices: /device:TPU:10 before, /device:TPU:3 now
where the time goes in v3:
time: 46.6 us; the launch traced here: 46.4 us
  Pallas kernels  44.7 us (96%)
  local copies, waits for them, and re-layouts  1.67 us (4%)
    pallas_call x1, Pallas kernels, per_device(): pl.pallas_call(functools.partial(kernel, (S, I, J, R, C, half, channels))...  44.7 us
    unnamed x1, local copies, waits for them, and re-layouts  1.67 us

profile of v3, /device:TPU:3, one launch (start us, length us, event | category | flops | bytes accessed | tf_op | source)
XLA Modules:
  0.0 46.4 jit_solution(11722926090485469720)
XLA Ops:
  0.0 44.7 %shard_map.82 = f32[512,128]{1,0:T(8,128)} custom-call(f32[1024,256]{1,0:T(8,128)} %bitcast.6, f32[512,128]{1,0:T(8,128)} %bitcast.7, f32[32,256]{1,0:T(8,128)} %bitcast.8, f32[32,256]{1,0:T(8,128)} %bitcast.9, f32[1024,128]{1,0:T(8,128)} %outer_hbm.1, f32[128,512]{1,0:T(8,128)} %tri_in_hbm.1, f32[128,128]{1,0:T(8,128)} %gate_w_hbm.1, f32[128,128]{1,0:T(8,128)} %tri_out_hbm.1), custom_call_target="tpu_custom_call" | custom-call | flops 1080000000 | bytes 3000000 | tf_op jit(solution)/shard_map/pallas_call | solution.py:574
  44.8 1.7 %copy.10 = f32[8,64,128]{2,1,0:T(8,128)} copy(f32[8,64,128]{2,1,0:T(8,128)} %bitcast.5) | data formatting | bytes 524288

commit v4 on v3

--- a/solution.py
+++ b/solution.py
@@ -22,10 +22,6 @@
 
 def dot_nn(a, b):
     return lax.dot_general(a, b, (((1,), (0,)), ((), ())), preferred_element_type=f32)
-
-
-def dot_nt(a, b):
-    return lax.dot_general(a, b, (((1,), (1,)), ((), ())), preferred_element_type=f32)
 
 
 def layer_norm(values):
@@ -59,6 +55,7 @@
     gate_w_ref,
     tri_out_ref,
     nm_ref,
+    left_ref,
     lt_ref,
     rt_ref,
     rg,
@@ -134,21 +131,19 @@
 
     for load in loads[:3]:
         load.wait()
-    both = jnp.concatenate([first_ref[...], second_ref[...]], 0)
-    both_h, both_l = split(both)
-    both_hl = jnp.concatenate([both_h, both_l], 0)
-    depth = msa_ref.shape[1]
-    normed = layer_norm(msa_ref[...])
-    for n in range(depth // 128):
-        nm_ref[n] = normed[:, n * 128 : (n + 1) * 128]
+    both_h, both_l = split(jnp.concatenate([first_ref[...], second_ref[...]], 0).T)
+    both_hl = jnp.concatenate([both_h, both_l], 1)
+    block = 256
+    for n in range(S * I // block):
+        sl = slice(n * block, (n + 1) * block)
+        xh, xl = split(layer_norm(msa_ref[sl, :]))
+        t = dot_nn(xh, both_hl)
+        t = t + dot_nn(xl, jnp.concatenate([both_h, jnp.zeros_like(both_h)], 1))
+        nm_ref[sl, :] = t + pltpu.roll(t, 2 * half, 1)
     for m in range(I):
-        xh, xl = split(
-            jnp.concatenate([nm_ref[n, pl.ds(m, S, stride=I), :] for n in range(depth // 128)], 1)
-        )
-        t = dot_nt(both_hl, xh)
-        t = t[: 2 * half] + t[2 * half :] + dot_nt(both_h, xl)
+        t = nm_ref[pl.ds(m, S, stride=I), :].T
         lt_ref[m * half : (m + 1) * half, :] = t[:half] * (1.0 / S)
-        rt_ref[m * half : (m + 1) * half, :] = t[half:]
+        rt_ref[m * half : (m + 1) * half, :] = t[half : 2 * half]
 
     @pl.when(lax.div(r, nr) == c)
     def _():
@@ -217,16 +212,18 @@
     for b in range(half):
         wp_ref[b * half : (b + 1) * half, :] = outer_ref[pl.ds(b, half, stride=half), :]
 
-    lt = lt_ref[...]
-    lt_h, lt_l = split(lt)
-    lt_hh = jnp.concatenate([lt_h, lt_h], 1)
+    lt_h, lt_l = split(lt_ref[...].T)
+    left_ref[:S, :] = lt_h
+    left_ref[S : 2 * S, :] = lt_h
+    left_ref[2 * S :, :] = lt_l
     lane = lax.broadcasted_iota(jnp.int32, (half // 4, I, 128), 2)
     low64 = lane < 64
     low32 = lax.rem(lane, 64) < 32
 
     def outer_block(slot):
         rh, rl = split(rg[slot])
-        o = dot_nt(jnp.concatenate([rh, rl], 1), lt_hh) + dot_nt(rh, lt_l)
+        o = dot_nn(jnp.concatenate([rh, rl], 1), left_ref[: 2 * S, :])
+        o = o + dot_nn(rh, left_ref[2 * S :, :])
         o = o.reshape(half // 4, 4, I, half * I)
         for h in range(half * I // 128):
             x = [o[:, q, :, h * 128 : (h + 1) * 128] for q in range(4)]
@@ -247,12 +244,13 @@
     w_hl = jnp.concatenate([wh, wl], 1)
     for load in loads[4:]:
         load.wait()
-    in_w = jnp.concatenate([tri_in_ref[...], gate_w_ref[...]], 1)
-    in_h, in_l = split(in_w)
+    ch = tri_out_ref.shape[0]
+    right_h, right_l = split(tri_in_ref[:, 2 * ch :])
+    right_hh = jnp.concatenate([right_h, right_h], 0)
+    in_h, in_l = split(jnp.concatenate([tri_in_ref[:, : 2 * ch], gate_w_ref[...]], 1))
     in_hh = jnp.concatenate([in_h, in_h], 0)
     out_h, out_l = split(tri_out_ref[...])
     out_hh = jnp.concatenate([out_h, out_h], 0)
-    ch = tri_out_ref.shape[0]
     group = 4 * 64
 
     def pair_group(zi):
@@ -271,8 +269,9 @@
         sl = pl.ds(pl.multiple_of(zi * group, group), group)
         pm_ref[sl, :] = mid
         nh, nl = split(layer_norm(mid))
-        pr = dot_nn(jnp.concatenate([nh, nl], 1), in_hh) + dot_nn(nh, in_l)
-        redge_ref[sl, :] = sigmoid(pr[:, 3 * ch : 4 * ch]) * pr[:, 2 * ch : 3 * ch]
+        nhl = jnp.concatenate([nh, nl], 1)
+        pr = dot_nn(nhl, right_hh) + dot_nn(nh, right_l)
+        redge_ref[sl, :] = sigmoid(pr[:, ch:]) * pr[:, :ch]
         for s in range(4):
             for k in range(I):
                 at = pl.multiple_of(zi * group + (s * I + k) * I, I)
@@ -281,10 +280,11 @@
                 ]
         for n in range(parts // zs):
             send_on(0, zi * (parts // zs) + n)
+        pr = dot_nn(nhl, in_hh) + dot_nn(nh, in_l)
         lall[2 * y + core, sl, :] = sigmoid(pr[:, ch : 2 * ch]) * pr[:, :ch]
         l_copy(0, zi).start()
         l_copy(1, zi).start()
-        gate_ref[sl, :] = sigmoid(pr[:, 4 * ch :])
+        gate_ref[sl, :] = sigmoid(pr[:, 2 * ch :])
 
     part = rows // parts
 
@@ -578,7 +578,8 @@
         out_specs=pl.BlockSpec(memory_space=pltpu.VMEM),
         scratch_shapes=[pltpu.VMEM(x.shape, f32) for x in operands]
         + [
-            pltpu.VMEM((depth // 128, S * I, 128), f32),
+            pltpu.VMEM((S * I, 4 * half), f32),
+            pltpu.VMEM((3 * S, I * half), bf16),
             pltpu.VMEM((I * half, S), f32),
             pltpu.VMEM((I * half, S), f32),
             pltpu.VMEM((nr, half * I, S), f32),

time: 46.6 us -> 47.3 us (1.015)
  Pallas kernels: 44.7 us -> 45.5 us
    pallas_call x1, Pallas kernels: 44.7 us -> 45.5 us  [per_device(): pl.pallas_call(functools.partial(kernel, (S, I, J, R, C, half, channels))...]
where the time goes in v4:
time: 47.3 us; the launch traced here: 47.2 us
  Pallas kernels  45.5 us (96%)
  local copies, waits for them, and re-layouts  1.67 us (4%)
    pallas_call x1, Pallas kernels, per_device(): pl.pallas_call(functools.partial(kernel, (S, I, J, R, C, half, channels))...  45.5 us
    unnamed x1, local copies, waits for them, and re-layouts  1.67 us

profile of v4, /device:TPU:3, one launch (start us, length us, event | category | flops | bytes accessed | tf_op | source)
XLA Modules:
  0.0 47.2 jit_solution(1544799928530644667)
XLA Ops:
  0.0 45.5 %shard_map.82 = f32[512,128]{1,0:T(8,128)} custom-call(f32[1024,256]{1,0:T(8,128)} %bitcast.6, f32[512,128]{1,0:T(8,128)} %bitcast.7, f32[32,256]{1,0:T(8,128)} %bitcast.8, f32[32,256]{1,0:T(8,128)} %bitcast.9, f32[1024,128]{1,0:T(8,128)} %outer_hbm.1, f32[128,512]{1,0:T(8,128)} %tri_in_hbm.1, f32[128,128]{1,0:T(8,128)} %gate_w_hbm.1, f32[128,128]{1,0:T(8,128)} %tri_out_hbm.1), custom_call_target="tpu_custom_call" | custom-call | flops 1080000000 | bytes 3000000 | tf_op jit(solution)/shard_map/pallas_call | solution.py:574
  45.5 1.7 %copy.10 = f32[8,64,128]{2,1,0:T(8,128)} copy(f32[8,64,128]{2,1,0:T(8,128)} %bitcast.5) | data formatting | bytes 524288

commit v5 on v3

--- a/solution.py
+++ b/solution.py
@@ -452,50 +452,65 @@
             a_across(t + 1)
         pair_group(zi)
 
-    for t in range(zs):
-        zi = turned(t, z)
-        l_arrived(2 * (1 - y) + core, zi)
-        l_copy(2, zi).start()
+    def pass_on(t, n):
+        below = part_order(z - t, n)
+        above = part_order(z + t, n)
+
+        @pl.when(z >= t)
+        def _():
+            line_up(t, below).wait_recv()
+
+            @pl.when(z < Z - 1)
+            def _():
+                line_up(t, below).start()
+
+        @pl.when(z + t < Z)
+        def _():
+            line_down(t, above).wait_recv()
+
+            @pl.when(z > 0)
+            def _():
+                line_down(t, above).start()
+
+    def add_up(t, n):
+        @pl.when(z >= t)
+        def _():
+            triangle(t, z - t, part_order(z - t, n), n == 0, n == parts - 1)
+
+        @pl.when(z + t < Z)
+        def _():
+            triangle(Z - 1 + t, z + t, part_order(z + t, n), n == 0, n == parts - 1)
+
+        if n == parts - 1:
+            if t == 1:
+                finish(z, z >= 0)
+            else:
+                finish(z - t + 1, z >= t - 1)
+                finish(z + t - 1, z + t - 1 < Z)
+
+    for n in range(parts):
+        pass_on(1, n)
+        if n < zs:
+            zi = turned(n, z)
+            l_arrived(2 * (1 - y) + core, zi)
+            l_copy(2, zi).start()
     for t in range(zs):
         zi = turned(t, z)
         l_arrived(2 * y + 1 - core, zi)
         l_arrived(2 * (1 - y) + 1 - core, zi)
     for n in range(parts):
         triangle(0, z, part_order(z, n), n == 0, n == parts - 1)
-    for t in range(1, Z):
-        for n in range(parts):
-            below = part_order(z - t, n)
-            above = part_order(z + t, n)
-
-            @pl.when(z >= t)
-            def _():
-                line_up(t, below).wait_recv()
-
-                @pl.when(z < Z - 1)
-                def _():
-                    line_up(t, below).start()
-
-            @pl.when(z + t < Z)
-            def _():
-                line_down(t, above).wait_recv()
-
-                @pl.when(z > 0)
-                def _():
-                    line_down(t, above).start()
-
-            @pl.when(z >= t)
-            def _():
-                triangle(t, z - t, below, n == 0, n == parts - 1)
-
-            @pl.when(z + t < Z)
-            def _():
-                triangle(Z - 1 + t, z + t, above, n == 0, n == parts - 1)
-
-        if t == 1:
-            finish(z, z >= 0)
-        else:
-            finish(z - t + 1, z >= t - 1)
-            finish(z + t - 1, z + t - 1 < Z)
+    todo = [(1, n) for n in range(parts)]
+    order = [(t, n) for t in range(2, Z) for n in range(parts)]
+    for step in order[:-1]:
+        add_up(*todo.pop(0))
+        pass_on(*step)
+        todo.append(step)
+    for step in todo:
+        add_up(*step)
+    for step in order[-1:]:
+        pass_on(*step)
+        add_up(*step)
     finish(z - Z + 1, z >= Z - 1)
     finish(z + Z - 1, z < 1)
 

time: 46.6 us -> 46.2 us (level)
  Pallas kernels: 44.7 us -> 44 us
    pallas_call x1, Pallas kernels: 44.7 us -> 44 us  [per_device(): pl.pallas_call(functools.partial(kernel, (S, I, J, R, C, half, channels))...]
where the time goes in v5:
time: 46.2 us; the launch traced here: 45.7 us
  Pallas kernels  44 us (95%)
  local copies, waits for them, and re-layouts  1.67 us (4%)
    pallas_call x1, Pallas kernels, per_device(): pl.pallas_call(functools.partial(kernel, (S, I, J, R, C, half, channels))...  44 us
    unnamed x1, local copies, waits for them, and re-layouts  1.67 us

profile of v5, /device:TPU:3, one launch (start us, length us, event | category | flops | bytes accessed | tf_op | source)
XLA Modules:
  0.0 45.7 jit_solution(16073962024662954045)
XLA Ops:
  0.0 44.0 %shard_map.82 = f32[512,128]{1,0:T(8,128)} custom-call(f32[1024,256]{1,0:T(8,128)} %bitcast.6, f32[512,128]{1,0:T(8,128)} %bitcast.7, f32[32,256]{1,0:T(8,128)} %bitcast.8, f32[32,256]{1,0:T(8,128)} %bitcast.9, f32[1024,128]{1,0:T(8,128)} %outer_hbm.1, f32[128,512]{1,0:T(8,128)} %tri_in_hbm.1, f32[128,128]{1,0:T(8,128)} %gate_w_hbm.1, f32[128,128]{1,0:T(8,128)} %tri_out_hbm.1), custom_call_target="tpu_custom_call" | custom-call | flops 1080000000 | bytes 3000000 | tf_op jit(solution)/shard_map/pallas_call | solution.py:589
  44.0 1.7 %copy.10 = f32[8,64,128]{2,1,0:T(8,128)} copy(f32[8,64,128]{2,1,0:T(8,128)} %bitcast.5) | data formatting | bytes 524288
